TPU v7x, 256 devices: a whole 4x4x8 slice. The times are simulated.
256 devices in a mesh: lat: 16 (over x_hi, y, core), lon: 16 (over x_lo, z).
Axes of the slice: x: 4 (x_hi: 2, x_lo: 2; x = x_hi * 2 + x_lo), y: 4, z: 8, core: 2. Of those that a mesh axis runs over, the one named last changes fastest.
Arguments:
- queries: bfloat16 [16, 32, 64, 1024], P('lat', 'lon'), may hold values from -36 to 36
- keys_values: bfloat16 [2, 16, 32, 64, 1024], P(None, 'lat', 'lon'), may hold values from -4 to 4
- cotangent: bfloat16 [16, 32, 64, 1024], P('lat', 'lon'), may hold values from -6 to 6
- blocks: int32 [16, 32, 6], P('lat', 'lon'), may hold values from 0 to 511, as said below
Outputs:
- attended: bfloat16 [16, 32, 64, 1024], P('lat', 'lon')
- grad_queries: bfloat16 [16, 32, 64, 1024], P('lat', 'lon')
- grad_keys_values: bfloat16 [2, 16, 32, 64, 1024], P(None, 'lat', 'lon')
Inputs may be any that keep to these rules, and one draw needn't show every extreme that they name: Entry 0 of each query block's list is the block itself. The other 5 entries are distinct blocks other than itself, whose band differs by at most one from the query block's band and whose sector differs by at most one, counted cyclically over 32 sectors.
All inputs are finite; a program needn't handle non-finite values.
Results may differ from a plain program's by a relative error of at most 0.0085.
Values may be sent and summed in bfloat16 or wider, within the bound.
A program may use at most 128 MiB of HBM per device.

v0:
```python
import jax
import jax.numpy as jnp
from jax import lax
from jax.sharding import PartitionSpec as P

HEADS = 16
HEAD_DIM = 64
D = 1024
CELLS = 64


def shifted(value, axis, steps):
    count = lax.axis_size(axis)
    pairs = [(source, (source + steps) % count) for source in range(count)]
    return lax.ppermute(value, axis, pairs)


def passed_along(value, axis, steps):
    count = lax.axis_size(axis)
    first, last = (max(0, -steps), min(count, count - steps))
    return lax.ppermute(value, axis, [(source, source + steps) for source in range(first, last)])


def extended_2(cells, sides, width, closed):
    for axis, dim in sides:
        count = lax.axis_size(axis)
        ends = count if closed else count - 1
        head = lax.slice_in_dim(cells, 0, width, axis=dim)
        tail = lax.slice_in_dim(cells, cells.shape[dim] - width, cells.shape[dim], axis=dim)
        cells = jnp.concatenate(
            [
                lax.ppermute(tail, axis, [(i, (i + 1) % count) for i in range(ends)]),
                cells,
                lax.ppermute(head, axis, [((i + 1) % count, i) for i in range(ends)]),
            ],
            axis=dim,
        )
    return cells


def band_attend(query_row, upstream_row, key_row, value_row, listed_row):
    scale = HEAD_DIM ** (-0.5)
    sector_cols = query_row.shape[0]
    query_heads = query_row.reshape(sector_cols, CELLS, HEADS, HEAD_DIM)
    upstream_heads = upstream_row.reshape(sector_cols, CELLS, HEADS, HEAD_DIM)
    key_heads = key_row.reshape(sector_cols, 9 * CELLS, HEADS, HEAD_DIM)
    value_heads = value_row.reshape(sector_cols, 9 * CELLS, HEADS, HEAD_DIM)
    keep = jnp.repeat(listed_row, CELLS, axis=1)[:, None, None, :]
    scores = (
        jnp.einsum("bihe,bjhe->bhij", query_heads, key_heads, preferred_element_type=jnp.float32)
        * scale
    )
    highest = jnp.max(jnp.where(keep, scores, -jnp.inf), axis=3, keepdims=True)
    raised = jnp.where(keep, jnp.exp(jnp.minimum(scores - highest, 0.0)), 0.0)
    total = jnp.sum(raised, axis=3, keepdims=True)
    weights = raised / total
    weights_low = weights.astype(jnp.bfloat16)
    attended = jnp.einsum(
        "bhij,bjhe->bihe", weights_low, value_heads, preferred_element_type=jnp.float32
    )
    attended = attended.reshape(sector_cols, CELLS, D).astype(jnp.bfloat16)
    pressure = jnp.einsum(
        "bihe,bjhe->bhij", upstream_heads, value_heads, preferred_element_type=jnp.float32
    )
    inner = jnp.sum(weights * pressure, axis=3, keepdims=True)
    score_grad = (weights * (pressure - inner) * scale).astype(jnp.bfloat16)
    grad_query = jnp.einsum(
        "bhij,bjhe->bihe", score_grad, key_heads, preferred_element_type=jnp.float32
    )
    grad_query = grad_query.reshape(sector_cols, CELLS, D).astype(jnp.bfloat16)
    grad_key = jnp.einsum(
        "bhij,bihe->bjhe", score_grad, query_heads, preferred_element_type=jnp.float32
    )
    grad_value = jnp.einsum(
        "bhij,bihe->bjhe", weights_low, upstream_heads, preferred_element_type=jnp.float32
    )
    stats = jnp.stack([highest[..., 0], total[..., 0], inner[..., 0]], axis=1)
    return (
        attended,
        grad_query,
        grad_key.reshape(sector_cols, 9, CELLS, D),
        grad_value.reshape(sector_cols, 9, CELLS, D),
        stats,
    )


def sector_section(grads, sector_cols):
    from_next = shifted(grads[:, :, 0].astype(jnp.bfloat16), "lon", -1).astype(jnp.float32)
    from_prior = shifted(grads[:, :, sector_cols + 1].astype(jnp.bfloat16), "lon", 1).astype(
        jnp.float32
    )
    grads = grads.at[:, :, sector_cols].add(from_next)
    grads = grads.at[:, :, 1].add(from_prior)
    return grads[:, :, 1 : sector_cols + 1]


def band_section(grads, band_rows):
    from_next = passed_along(grads[:, 0], "lat", -1)
    from_prior = passed_along(grads[:, band_rows + 1], "lat", 1)
    grads = grads.at[:, band_rows].add(from_next)
    grads = grads.at[:, 1].add(from_prior)
    return grads[:, 1 : band_rows + 1]


def body(queries, keys_values, cotangent, blocks):
    band_rows = queries.shape[0]
    sector_cols = queries.shape[1]
    sector_total = sector_cols * lax.axis_size("lon")
    extended = extended_2(keys_values, (("lat", 1),), 1, False)
    extended = extended_2(extended, (("lon", 2),), 1, True)
    ext_rows = band_rows + 2
    ext_cols = sector_cols + 2
    lat_index = lax.axis_index("lat")
    lon_index = lax.axis_index("lon")
    band_index = blocks // sector_total
    sector_index = blocks % sector_total
    local_row = band_index - lat_index * band_rows + 1
    local_col = (sector_index - lon_index * sector_cols + 1) % sector_total
    relative = (local_row - jnp.arange(band_rows, dtype=jnp.int32)[:, None, None]) * 3 + (
        local_col - jnp.arange(sector_cols, dtype=jnp.int32)[None, :, None]
    )
    listed = jnp.any(relative[..., None] == jnp.arange(9, dtype=jnp.int32), axis=2)
    grads = jnp.zeros((2, ext_rows, ext_cols, CELLS, D), jnp.float32)
    stat_rows = []
    key_row = jnp.concatenate(
        [extended[0, dr, dc : dc + sector_cols] for dr in range(3) for dc in range(3)], axis=1
    )
    value_row = jnp.concatenate(
        [extended[1, dr, dc : dc + sector_cols] for dr in range(3) for dc in range(3)], axis=1
    )
    attended_row, grad_row, grad_key, grad_value, stats = band_attend(
        queries[0], cotangent[0], key_row, value_row, listed[0]
    )
    for offset in range(9):
        dr = offset // 3
        dc = offset % 3
        grads = grads.at[0, dr, dc : dc + sector_cols].add(grad_key[:, offset])
        grads = grads.at[1, dr, dc : dc + sector_cols].add(grad_value[:, offset])
    attended_rows = [attended_row]
    grad_rows = [grad_row]
    stat_rows.append(stats)
    grads = band_section(sector_section(grads, sector_cols), band_rows)
    attended = jnp.stack(attended_rows)
    grad_queries = jnp.stack(grad_rows)
    return (attended, grad_queries, grads.astype(jnp.bfloat16))


def solution(mesh):
    placed = (
        P("lat", "lon", None, None),
        P(None, "lat", "lon", None, None),
        P("lat", "lon", None, None),
        P("lat", "lon", None),
    )
    return jax.shard_map(
        body,
        mesh=mesh,
        in_specs=placed,
        out_specs=(
            P("lat", "lon", None, None),
            P("lat", "lon", None, None),
            P(None, "lat", "lon", None, None),
        ),
        check_vma=False,
    )
```

profile of v0, /device:TPU:25, one launch (start us, length us, event | category | flops | bytes accessed | tf_op | source)
XLA Modules:
  0.0 211.6 jit_solution(15327527825104180510)
XLA Ops:
  0.7 5.0 %collective-permute-start = (bf16[2,1,2,64,1024]{4,3,2,1,0:T(8,128)(2,1)}, bf16[2,1,2,64,1024]{4,3,2,1,0:T(8,128)(2,1)S(1)}, u32[]{:S(2)}, u32[]{:S(2)}) collective-permute-start(bf16[2,1,2,64,1024]{4,3,2,1,0:T(8,128)(2,1)} %param.49), channel_id=1, source_target_pairs={{0,16},{16,32},{32,48},{48,64},{64,80},{80,96},{96,112},{112,128},... | collective-permute-start | bytes 1572872 | tf_op jit(solution)/shard_map/ppermute | solution.py:32
  5.7 1.9 collective-permute-start.1
  7.6 1.8 fusion.77
  9.4 2.7 %collective-permute-done = bf16[2,1,2,64,1024]{4,3,2,1,0:T(8,128)(2,1)S(1)} collective-permute-done((bf16[2,1,2,64,1024]{4,3,2,1,0:T(8,128)(2,1)}, bf16[2,1,2,64,1024]{4,3,2,1,0:T(8,128)(2,1)S(1)}, u32[]{:S(2)}, u32[]{:S(2)}) %collective-permute-start) | collective-permute-done | bytes 524320 | tf_op jit(solution)/shard_map/ppermute | solution.py:32
  12.1 1.1 constant_dynamic-update-slice_fusion.1
  13.2 6.8 %collective-permute-done.1 = bf16[2,1,2,64,1024]{4,3,2,1,0:T(8,128)(2,1)S(1)} collective-permute-done((bf16[2,1,2,64,1024]{4,3,2,1,0:T(8,128)(2,1)}, bf16[2,1,2,64,1024]{4,3,2,1,0:T(8,128)(2,1)S(1)}, u32[]{:S(2)}, u32[]{:S(2)}) %collective-permute-start.1) | collective-permute-done | bytes 524320 | tf_op jit(solution)/shard_map/ppermute | solution.py:34
  20.0 1.4 fusion.75
  21.4 5.6 %collective-permute-start.3 = (bf16[2,3,1,64,1024]{4,3,2,1,0:T(8,128)(2,1)}, bf16[2,3,1,64,1024]{4,3,2,1,0:T(8,128)(2,1)}, u32[]{:S(2)}, u32[]{:S(2)}) collective-permute-start(bf16[2,3,1,64,1024]{4,3,2,1,0:T(8,128)(2,1)} %get-tuple-element.292), channel_id=1, source_target_pairs={{1,0},{2,1},{3,2},{4,3},{5,4},{6,5},{7,6},{8,7},{9,8},{10,9},{11,1... | collective-permute-start | bytes 2359304 | tf_op jit(solution)/shard_map/ppermute | solution.py:34
  27.4 1.0 copy.169
  29.4 1.2 copy.114
  30.6 1.0 copy.105
  33.1 2.0 copy.117
  35.0 1.0 copy.108
  36.1 1.0 copy.111
  37.1 1.0 copy.102
  38.1 2.0 collective-permute-done.3
  40.1 2.0 pad_maximum_fusion
  42.1 2.0 copy.118
  46.1 1.0 copy.109
  47.1 1.0 copy.106
  49.2 2.0 pad_maximum_fusion.1
  51.2 2.0 copy.116
  53.2 1.0 copy.113
  55.2 1.0 copy.107
  56.2 1.0 copy.104
  58.3 5.3 %concatenate.151 = bf16[2,576,16,64]{1,3,2,0:T(8,128)(2,1)S(1)} concatenate(bf16[2,64,16,64]{1,3,2,0:T(8,128)(2,1)} %bitcast.291, bf16[2,64,16,64]{1,3,2,0:T(8,128)(2,1)} %bitcast.279, bf16[2,64,16,64]{1,3,2,0:T(8,128)(2,1)} %bitcast.285, bf16[2,64,16,64]{1,3,2,0:T(8,128)(2,1)} %bitcast.290, bf16[2,64,16,64]{1,3,2,0:T(8,128)(2,1)} %bitcast.275, ...), dimensions={1} | concatenate | bytes 4718592 | tf_op jit(solution)/shard_map/concatenate | solution.py:128
  63.6 4.3 %fusion.80 = f32[2,16,576,64]{2,3,1,0:T(8,128)} fusion(bf16[2,64,16,64]{1,3,2,0:T(8,128)(2,1)} %bitcast.292, bf16[2,576,16,64]{1,3,2,0:T(8,128)(2,1)S(1)} %concatenate.151), kind=kOutput, calls=%fused_computation.133 | convolution fusion | flops 150994944 | bytes 7340032 | tf_op jit(solution)/shard_map/bihe,bjhe->bhij/dot_general | solution.py:62
  67.9 6.7 %concatenate.161 = bf16[2,576,16,64]{1,3,2,0:T(8,128)(2,1)} concatenate(bf16[2,64,16,64]{1,3,2,0:T(8,128)(2,1)} %bitcast.288, bf16[2,64,16,64]{1,3,2,0:T(8,128)(2,1)} %bitcast.277, bf16[2,64,16,64]{1,3,2,0:T(8,128)(2,1)} %bitcast.282, bf16[2,64,16,64]{1,3,2,0:T(8,128)(2,1)} %bitcast.287, bf16[2,64,16,64]{1,3,2,0:T(8,128)(2,1)S(1)} %bitcast.274, ...), dimensions={1} | concatenate | bytes 4718592 | tf_op jit(solution)/shard_map/concatenate | solution.py:125
  74.6 7.6 %bitcast_reduce_fusion = (f32[2,16,64]{2,1,0:T(8,128)S(1)}, f32[2,16,576,64]{2,3,1,0:T(8,128)}) fusion(pred[2,576]{1,0:T(4,128)(4,1)S(1)} %broadcast_in_dim.31, bf16[2,64,16,64]{1,3,2,0:T(8,128)(2,1)} %bitcast.294, bf16[2,576,16,64]{1,3,2,0:T(8,128)(2,1)} %concatenate.161), kind=kOutput, calls=%fused_computation.8 | convolution fusion | flops 310248000 | bytes 7349376 | tf_op jit(solution)/shard_map/sub | solution.py:54
  82.2 5.8 %convolution_bitcast_fusion = f32[2,576,16,64]{1,3,2,0:T(8,128)} fusion(bf16[2,64,16,64]{1,3,2,0:T(8,128)(2,1)S(1)} %bitcast.293, f32[2,16,576,64]{2,3,1,0:T(8,128)} %get-tuple-element.304, f32[2,16,64]{2,1,0:T(8,128)S(1)} %get-tuple-element.303), kind=kOutput, calls=%fused_computation.16 | convolution fusion | flops 153354240 | bytes 9707520 | tf_op jit(solution)/shard_map/bhij,bihe->bjhe/dot_general | solution.py:74
  88.0 21.4 %convolution_bitcast_fusion.1 = f32[2,576,16,64]{1,3,2,0:T(8,128)} fusion(bf16[2,64,16,64]{1,3,2,0:T(8,128)(2,1)} %bitcast.295, f32[2,16,576,64]{2,3,1,0:T(8,128)} %fusion.80, f32[2,16,576,64]{2,3,1,0:T(8,128)} %get-tuple-element.304, f32[2,16,64]{2,1,0:T(8,128)S(1)} %get-tuple-element.303), kind=kOutput, calls=%fused_computation.17 | convolution fusion | flops 159255104 | bytes 14426112 | tf_op jit(solution)/shard_map/bhij,bihe->bjhe/dot_general | solution.py:71
  109.4 8.5 %copy.125 = f32[2,576,16,64]{3,2,1,0:T(8,128)} copy(f32[2,576,16,64]{1,3,2,0:T(8,128)} %convolution_bitcast_fusion) | data formatting | bytes 9437184 | tf_op jit(solution)/shard_map/bhij,bihe->bjhe/transpose | solution.py:74
  117.9 8.9 %reshape.1034 = f32[2,9,64,1024]{3,2,1,0:T(8,128)} reshape(f32[2,576,16,64]{3,2,1,0:T(8,128)} %copy.125) | data formatting | bytes 9437184 | tf_op jit(solution)/shard_map/reshape | solution.py:82
  126.8 8.5 %copy.122 = f32[2,576,16,64]{3,2,1,0:T(8,128)} copy(f32[2,576,16,64]{1,3,2,0:T(8,128)} %convolution_bitcast_fusion.1) | data formatting | bytes 9437184 | tf_op jit(solution)/shard_map/bhij,bihe->bjhe/transpose | solution.py:71
  135.3 8.9 %reshape.1033 = f32[2,9,64,1024]{3,2,1,0:T(8,128)} reshape(f32[2,576,16,64]{3,2,1,0:T(8,128)} %copy.122) | data formatting | bytes 9437184 | tf_op jit(solution)/shard_map/reshape | solution.py:81
  144.2 1.2 slice_bitcast_fusion.22
  146.8 1.6 fusion.59
  149.4 2.0 fusion.43
  152.7 4.1 %collective-permute-start.4 = (bf16[2,3,64,1024]{3,2,1,0:T(8,128)(2,1)S(1)}, bf16[2,3,64,1024]{3,2,1,0:T(8,128)(2,1)S(1)}, u32[]{:S(2)}, u32[]{:S(2)}) collective-permute-start(bf16[2,3,64,1024]{3,2,1,0:T(8,128)(2,1)S(1)} %get-tuple-element.279), channel_id=1, source_target_pairs={{0,15},{1,0},{2,1},{3,2},{4,3},{5,4},{6,5},{7,6},{8,7},{9,8},{10,9... | collective-permute-start | bytes 2359304 | tf_op jit(solution)/shard_map/ppermute | solution.py:15
  156.8 1.1 copy.142
  157.9 12.7 %collective-permute-done.4 = bf16[2,3,64,1024]{3,2,1,0:T(8,128)(2,1)S(1)} collective-permute-done((bf16[2,3,64,1024]{3,2,1,0:T(8,128)(2,1)S(1)}, bf16[2,3,64,1024]{3,2,1,0:T(8,128)(2,1)S(1)}, u32[]{:S(2)}, u32[]{:S(2)}) %collective-permute-start.4) | collective-permute-done | bytes 786464 | tf_op jit(solution)/shard_map/ppermute | solution.py:15
  171.0 4.0 %collective-permute-done.5 = bf16[2,3,64,1024]{3,2,1,0:T(8,128)(2,1)S(1)} collective-permute-done((bf16[2,3,64,1024]{3,2,1,0:T(8,128)(2,1)S(1)}, bf16[2,3,64,1024]{3,2,1,0:T(8,128)(2,1)S(1)}, u32[]{:S(2)}, u32[]{:S(2)}) %collective-permute-start.5) | collective-permute-done | bytes 786464 | tf_op jit(solution)/shard_map/ppermute | solution.py:15
  175.4 1.7 slice_bitcast_fusion.1
  177.1 1.9 collective-permute-start.6
  179.0 7.3 %collective-permute-start.7 = (f32[2,2,64,1024]{3,2,1,0:T(8,128)}, f32[2,2,64,1024]{3,2,1,0:T(8,128)}, u32[]{:S(2)}, u32[]{:S(2)}) collective-permute-start(f32[2,2,64,1024]{3,2,1,0:T(8,128)} %get-tuple-element.277), channel_id=1, source_target_pairs={{0,16},{16,32},{32,48},{48,64},{64,80},{80,96},{96,112},{112,128},... | collective-permute-start | bytes 3145736 | tf_op jit(solution)/shard_map/ppermute | solution.py:21
  186.3 1.1 fusion.21
  188.3 19.5 %fusion.20 = bf16[2,16,64,64]{3,2,1,0:T(8,128)(2,1)S(1)} fusion(bf16[2,576,16,64]{1,3,2,0:T(8,128)(2,1)} %concatenate.161, f32[2,16,576,64]{2,3,1,0:T(8,128)} %fusion.80, f32[2,16,576,64]{2,3,1,0:T(8,128)} %get-tuple-element.304, f32[2,16,64]{2,1,0:T(8,128)S(1)} %get-tuple-element.303), kind=kOutput, calls=%fused_computation.28 | convolution fusion | flops 159386176 | bytes 12066816 | tf_op jit(solution)/shard_map/bhij,bjhe->bihe/dot_general | solution.py:67
  208.7 2.9 %fusion.27 = bf16[2,1,2,64,1024]{4,3,2,1,0:T(8,128)(2,1)} fusion(f32[2,2,64,1024]{3,2,1,0:T(8,128)} %collective-permute-done.7, f32[2,2,64,1024]{3,2,1,0:T(8,128)} %collective-permute-done.6, f32[2,3,4,64,1024]{4,3,2,1,0:T(8,128)} %copy-done), kind=kLoop, calls=%fused_computation.38 | loop fusion | flops 786432 | bytes 3670016
  (61 shorter events, 14.1 us)
Async XLA Ops:
  0.6 26.4 %copy-start.6 = (s32[1,2,6]{2,1,0:T(2,128)S(1)}, s32[1,2,6]{2,1,0:T(2,128)}, u32[]{:S(2)}) copy-start(s32[1,2,6]{2,1,0:T(2,128)} %param.51) | copy-start | bytes 148
  0.6 26.7 %copy-start.4 = (bf16[1,2,64,1024]{3,2,1,0:T(8,128)(2,1)S(1)}, bf16[1,2,64,1024]{3,2,1,0:T(8,128)(2,1)}, u32[]{:S(2)}) copy-start(bf16[1,2,64,1024]{3,2,1,0:T(8,128)(2,1)} %param.48) | copy-start | bytes 786436
  0.7 27.7 %copy-start.5 = (bf16[1,2,64,1024]{3,2,1,0:T(8,128)(2,1)S(1)}, bf16[1,2,64,1024]{3,2,1,0:T(8,128)(2,1)}, u32[]{:S(2)}) copy-start(bf16[1,2,64,1024]{3,2,1,0:T(8,128)(2,1)} %param.50) | copy-start | bytes 786436
  0.7 11.4 %collective-permute-start = (bf16[2,1,2,64,1024]{4,3,2,1,0:T(8,128)(2,1)}, bf16[2,1,2,64,1024]{4,3,2,1,0:T(8,128)(2,1)S(1)}, u32[]{:S(2)}, u32[]{:S(2)}) collective-permute-start(bf16[2,1,2,64,1024]{4,3,2,1,0:T(8,128)(2,1)} %param.49), channel_id=1, source_target_pairs={{0,16},{16,32},{32,48},{48,64},{64,80},{80,96},{96,112},{112,128},... | collective-permute-start | bytes 1572872 | tf_op jit(solution)/shard_map/ppermute | solution.py:32
  5.7 14.3 %collective-permute-start.1 = (bf16[2,1,2,64,1024]{4,3,2,1,0:T(8,128)(2,1)}, bf16[2,1,2,64,1024]{4,3,2,1,0:T(8,128)(2,1)S(1)}, u32[]{:S(2)}, u32[]{:S(2)}) collective-permute-start(bf16[2,1,2,64,1024]{4,3,2,1,0:T(8,128)(2,1)} %param.49), channel_id=1, source_target_pairs={{16,0},{32,16},{48,32},{64,48},{80,64},{96,80},{112,96},{128,112},... | collective-permute-start | bytes 1572872 | tf_op jit(solution)/shard_map/ppermute | solution.py:34
  21.4 18.7 %collective-permute-start.3 = (bf16[2,3,1,64,1024]{4,3,2,1,0:T(8,128)(2,1)}, bf16[2,3,1,64,1024]{4,3,2,1,0:T(8,128)(2,1)}, u32[]{:S(2)}, u32[]{:S(2)}) collective-permute-start(bf16[2,3,1,64,1024]{4,3,2,1,0:T(8,128)(2,1)} %get-tuple-element.292), channel_id=1, source_target_pairs={{1,0},{2,1},{3,2},{4,3},{5,4},{6,5},{7,6},{8,7},{9,8},{10,9},{11,1... | collective-permute-start | bytes 2359304 | tf_op jit(solution)/shard_map/ppermute | solution.py:34
  27.0 22.1 %collective-permute-start.2 = (bf16[2,3,1,64,1024]{4,3,2,1,0:T(8,128)(2,1)}, bf16[2,3,1,64,1024]{4,3,2,1,0:T(8,128)(2,1)}, u32[]{:S(2)}, u32[]{:S(2)}) collective-permute-start(bf16[2,3,1,64,1024]{4,3,2,1,0:T(8,128)(2,1)} %get-tuple-element.293), channel_id=1, source_target_pairs={{0,1},{1,2},{2,3},{3,4},{4,5},{5,6},{6,7},{7,8},{8,9},{9,10},{10,1... | collective-permute-start | bytes 2359304 | tf_op jit(solution)/shard_map/ppermute | solution.py:32
  74.6 7.6 %copy-start.3 = (bf16[1,2,64,1024]{2,3,1,0:T(8,128)(2,1)S(1)}, bf16[1,2,64,1024]{2,3,1,0:T(8,128)(2,1)}, u32[]{:S(2)}) copy-start(bf16[1,2,64,1024]{2,3,1,0:T(8,128)(2,1)} %copy.170) | copy-start | bytes 786436
  144.2 2.5 %copy-start.1 = (f32[2,9,64,1024]{3,2,1,0:T(8,128)S(1)}, f32[2,9,64,1024]{3,2,1,0:T(8,128)}, u32[]{:S(2)}) copy-start(f32[2,9,64,1024]{3,2,1,0:T(8,128)} %reshape.1034) | copy-start | bytes 14155780
  145.4 3.0 %copy-start.2 = (f32[2,9,64,1024]{3,2,1,0:T(8,128)S(1)}, f32[2,9,64,1024]{3,2,1,0:T(8,128)}, u32[]{:S(2)}) copy-start(f32[2,9,64,1024]{3,2,1,0:T(8,128)} %reshape.1033) | copy-start | bytes 14155780
  152.7 17.9 %collective-permute-start.4 = (bf16[2,3,64,1024]{3,2,1,0:T(8,128)(2,1)S(1)}, bf16[2,3,64,1024]{3,2,1,0:T(8,128)(2,1)S(1)}, u32[]{:S(2)}, u32[]{:S(2)}) collective-permute-start(bf16[2,3,64,1024]{3,2,1,0:T(8,128)(2,1)S(1)} %get-tuple-element.279), channel_id=1, source_target_pairs={{0,15},{1,0},{2,1},{3,2},{4,3},{5,4},{6,5},{7,6},{8,7},{9,8},{10,9... | collective-permute-start | bytes 2359304 | tf_op jit(solution)/shard_map/ppermute | solution.py:15
  156.8 18.1 %collective-permute-start.5 = (bf16[2,3,64,1024]{3,2,1,0:T(8,128)(2,1)S(1)}, bf16[2,3,64,1024]{3,2,1,0:T(8,128)(2,1)S(1)}, u32[]{:S(2)}, u32[]{:S(2)}) collective-permute-start(bf16[2,3,64,1024]{3,2,1,0:T(8,128)(2,1)S(1)} %get-tuple-element.278), channel_id=1, source_target_pairs={{0,1},{1,2},{2,3},{3,4},{4,5},{5,6},{6,7},{7,8},{8,9},{9,10},{10,1... | collective-permute-start | bytes 2359304 | tf_op jit(solution)/shard_map/ppermute | solution.py:15
  157.9 28.3 %slice-start = ((s8[5242880]{0:T(1024)(128)(4,1)}), s8[1048576]{0:T(1024)(128)(4,1)S(1)}, s32[]{:S(2)}) async-start(s8[5242880]{0:T(1024)(128)(4,1)} %bitcast.298), calls=%async_computation | async-start | bytes 2097152
  171.0 15.3 %slice-start.1 = ((s8[5242880]{0:T(1024)(128)(4,1)}), s8[4194304]{0:T(1024)(128)(4,1)S(1)}, s32[]{:S(2)}) async-start(s8[5242880]{0:T(1024)(128)(4,1)} %bitcast.298), calls=%async_computation.1 | async-start | bytes 8388608
  175.4 12.0 %copy-start = (f32[2,3,4,64,1024]{4,3,2,1,0:T(8,128)}, f32[2,3,4,64,1024]{4,3,2,1,0:T(8,128)S(1)}, u32[]{:S(2)}) copy-start(f32[2,3,4,64,1024]{4,3,2,1,0:T(8,128)S(1)} %fusion.14) | copy-start | bytes 18874372
  177.1 31.6 %collective-permute-start.6 = (f32[2,2,64,1024]{3,2,1,0:T(8,128)}, f32[2,2,64,1024]{3,2,1,0:T(8,128)}, u32[]{:S(2)}, u32[]{:S(2)}) collective-permute-start(f32[2,2,64,1024]{3,2,1,0:T(8,128)} %get-tuple-element.276), channel_id=1, source_target_pairs={{16,0},{32,16},{48,32},{64,48},{80,64},{96,80},{112,96},{128,112},... | collective-permute-start | bytes 3145736 | tf_op jit(solution)/shard_map/ppermute | solution.py:21
  179.0 29.7 %collective-permute-start.7 = (f32[2,2,64,1024]{3,2,1,0:T(8,128)}, f32[2,2,64,1024]{3,2,1,0:T(8,128)}, u32[]{:S(2)}, u32[]{:S(2)}) collective-permute-start(f32[2,2,64,1024]{3,2,1,0:T(8,128)} %get-tuple-element.277), channel_id=1, source_target_pairs={{0,16},{16,32},{32,48},{48,64},{64,80},{80,96},{96,112},{112,128},... | collective-permute-start | bytes 3145736 | tf_op jit(solution)/shard_map/ppermute | solution.py:21
where the time goes:
time: 214 us; the launch traced here: 212 us
  local copies, waits for them, and re-layouts  83.5 us (39%)
  matrix products  59.7 us (28%)
  waiting for transfers between devices  28.1 us (13%)
  starting transfers between devices  25.9 us (12%)
  other arithmetic  13.4 us (6%)
    dot_general x1, matrix products, band_attend(): jnp.einsum('bhij,bihe->bjhe', score_grad, query_heads, preferred_element_...  21.4 us
    dot_general x1, matrix products, band_attend(): jnp.einsum('bhij,bjhe->bihe', score_grad, key_heads, preferred_element_ty...  19.5 us
    ppermute x2, waiting for transfers between devices, shifted(): return lax.ppermute(value, axis, pairs)  16.7 us
    slice x12, local copies, waits for them, and re-layouts, body(): extended[0, dr, dc:dc + sector_cols]  14.7 us
    slice x9, local copies, waits for them, and re-layouts, body(): extended[1, dr, dc:dc + sector_cols]  9.2 us
    ppermute x2, starting transfers between devices, passed_along(): lax.ppermute(value, axis, [(source, source + steps) for source in range(f...  9.17 us
    reshape x1, local copies, waits for them, and re-layouts, band_attend(): grad_value.reshape(sector_cols, 9, CELLS, D)  8.88 us
    reshape x1, local copies, waits for them, and re-layouts, band_attend(): grad_key.reshape(sector_cols, 9, CELLS, D)  8.86 us
  transfers between devices with their start and end apart: 8, of which 5 were waited for; matrix products, arithmetic and copies ran while one was open for 22% of the time, Pallas kernels for 0%

commit v1 on v0

v1 whole, which is shorter than its diff:
```python
import jax
import jax.numpy as jnp
from jax import lax
from jax.experimental import pallas as pl
from jax.experimental.pallas import tpu as pltpu
from jax.sharding import PartitionSpec as P

HEAD_DIM = 64
CELLS = 64
D = 1024
CH = 256
NC = D // CH
PER = CH // HEAD_DIM
SECTORS = 2
SAMPLES = 6
OUTER, OWN, INNER = 0, 1, 2
HIDE = -1e30


def dot(a, b, ca, cb):
    return lax.dot_general(a, b, (((ca,), (cb,)), ((), ())), preferred_element_type=jnp.float32)


def make_kernel(n_lat, n_lon):
    sector_total = n_lon * SECTORS

    def kernel(
        blocks, q_hbm, kv_hbm, do_hbm, att_hbm, gq_hbm, gkv_hbm,
        ext, qs, dos, att_s, gq_s, gkv_s, g_own, g_out, g_halo,
        s_ic, s_oc, s_in, s_out, s_halo, r_ic, r_oc, r_in, r_out, r_halo,
        send_sem, recv_sem, load_sem, store_sem,
    ):
        i = lax.axis_index("lat")
        j = lax.axis_index("lon")
        core = lax.rem(i, 2)
        partner = i + 1 - 2 * core
        outer = lax.rem(i + 2 * core - 1 + n_lat, n_lat)
        left = lax.rem(j + n_lon - 1, n_lon)
        right = lax.rem(j + 1, n_lon)

        def cols(t):
            return pl.ds(pl.multiple_of(t * CH, CH), CH)

        def loads(t):
            return [
                pltpu.make_async_copy(kv_hbm.at[:, 0, :, :, cols(t)], ext.at[t, :, OWN, 1:3], load_sem.at[t, 0]),
                pltpu.make_async_copy(q_hbm.at[0, :, :, cols(t)], qs.at[t], load_sem.at[t, 1]),
                pltpu.make_async_copy(do_hbm.at[0, :, :, cols(t)], dos.at[t], load_sem.at[t, 2]),
            ]

        def stores(t):
            return [
                pltpu.make_async_copy(att_s.at[t], att_hbm.at[0, :, :, cols(t)], store_sem.at[t, 0]),
                pltpu.make_async_copy(gq_s.at[t], gq_hbm.at[0, :, :, cols(t)], store_sem.at[t, 1]),
                pltpu.make_async_copy(gkv_s.at[t], gkv_hbm.at[:, 0, :, :, cols(t)], store_sem.at[t, 2]),
            ]

        def remote(t, kind, src, dst, device):
            return pltpu.make_async_remote_copy(
                src_ref=src, dst_ref=dst, send_sem=send_sem.at[t, kind], recv_sem=recv_sem.at[t, kind],
                device_id=device, device_id_type=pl.DeviceIdType.MESH,
            )

        def to_lat(where):
            return (where, j)

        def to_lon(where):
            return (i, where)

        def first(t):
            return [
                remote(t, 0, kv_hbm.at[:, 0, :, :, cols(t)], ext.at[t, :, OUTER, 1:3], to_lat(outer)),
                remote(t, 1, kv_hbm.at[:, 0, 0, :, cols(t)], ext.at[t, :, OWN, 3], to_lon(left)),
                remote(t, 2, kv_hbm.at[:, 0, 1, :, cols(t)], ext.at[t, :, OWN, 0], to_lon(right)),
                remote(t, 3, kv_hbm.at[:, 0, :, :, cols(t)], ext.at[t, :, INNER, 1:3], to_lat(partner)),
            ]

        def second(t):
            return [
                remote(t, 4, ext.at[t, :, OUTER, 1], ext.at[t, :, OUTER, 3], to_lon(left)),
                remote(t, 5, ext.at[t, :, OUTER, 2], ext.at[t, :, OUTER, 0], to_lon(right)),
                remote(t, 6, ext.at[t, :, OWN, 3], ext.at[t, :, INNER, 3], to_lat(partner)),
                remote(t, 7, ext.at[t, :, OWN, 0], ext.at[t, :, INNER, 0], to_lat(partner)),
            ]

        def third(t):
            return [
                remote(t, 8, s_oc.at[t, 0], r_oc.at[t, 0], to_lon(left)),
                remote(t, 9, s_oc.at[t, 1], r_oc.at[t, 1], to_lon(right)),
                remote(t, 10, s_ic.at[t], r_ic.at[t], to_lat(partner)),
                remote(t, 11, s_in.at[t], r_in.at[t], to_lat(partner)),
            ]

        def fourth(t):
            return [
                remote(t, 12, s_out.at[t], r_out.at[t], to_lat(outer)),
                remote(t, 13, s_halo.at[t, 0], r_halo.at[t, 0], to_lon(left)),
                remote(t, 14, s_halo.at[t, 1], r_halo.at[t, 1], to_lon(right)),
            ]

        def start(copies):
            for copy in copies:
                copy.start()

        def forward(t):
            a, from_right, from_left, _ = first(t)
            to_left, to_right, right_in, left_in = second(t)
            from_right.wait_recv()
            right_in.start()
            from_left.wait_recv()
            left_in.start()
            a.wait_recv()
            to_left.start()
            to_right.start()

        sign = 1 - 2 * core
        bias = []
        for b in range(SECTORS):
            codes = []
            for s in range(SAMPLES):
                block = blocks[0, b, s]
                band = block // sector_total
                sector = block % sector_total
                column = (sector - (SECTORS * j + b) + 1 + sector_total) % sector_total
                codes.append((1 + sign * (band - i)) * 3 + column)
            row = []
            for o in range(9):
                listed = codes[0] == o
                for code in codes[1:]:
                    listed = listed | (code == o)
                row.append(jnp.where(listed, 0.0, HIDE).astype(jnp.float32))
            bias.append(row)

        head = lax.broadcasted_iota(jnp.int32, (CELLS, CH), 1) // HEAD_DIM
        on = [jnp.where(head == h, 1.0, 0.0).astype(jnp.float32) for h in range(PER)]
        on_low = [o.astype(jnp.bfloat16) for o in on]

        def spread(x):
            return jnp.concatenate([x * m for m in on_low], axis=0)

        def gathered(x):
            total = x[0:CELLS] * on[0]
            for h in range(1, PER):
                total = total + x[h * CELLS : (h + 1) * CELLS] * on[h]
            return total

        def compute(t):
            scale = HEAD_DIM ** -0.5
            grads = ([], [])
            for b in range(SECTORS):
                qbd = spread(qs[t, b])
                dbd = spread(dos[t, b])
                keys = ext[t, 0, :, b : b + 3].reshape(9 * CELLS, CH)
                values = ext[t, 1, :, b : b + 3].reshape(9 * CELLS, CH)
                scores = dot(keys, qbd, 1, 1)
                scores = jnp.concatenate(
                    [scores[o * CELLS : (o + 1) * CELLS] + bias[b][o] for o in range(9)], axis=0
                )
                highest = jnp.max(scores, axis=0, keepdims=True)
                raised = jnp.exp((scores - highest) * scale)
                weights = raised * (1.0 / jnp.sum(raised, axis=0, keepdims=True))
                low = weights.astype(jnp.bfloat16)
                pressure = dot(values, dbd, 1, 1)
                inner = jnp.sum(weights * pressure, axis=0, keepdims=True)
                score_grad = (weights * (pressure - inner) * scale).astype(jnp.bfloat16)
                att_s[t, b] = gathered(dot(low, values, 0, 0)).astype(jnp.bfloat16)
                gq_s[t, b] = gathered(dot(score_grad, keys, 0, 0)).astype(jnp.bfloat16)
                grads[0].append(dot(score_grad, qbd, 1, 0).reshape(3, 3, CELLS, CH))
                grads[1].append(dot(low, dbd, 1, 0).reshape(3, 3, CELLS, CH))
            for kv in range(2):
                g0, g1 = grads[kv]
                middle = [[g0[r, 1] + g1[r, 0], g0[r, 2] + g1[r, 1]] for r in range(3)]
                edges = [[g0[r, 0], g1[r, 2]] for r in range(3)]
                for side in range(2):
                    s_oc[t, side, kv] = edges[OUTER][side].astype(jnp.bfloat16)
                    s_ic[t, side, kv] = edges[INNER][side].astype(jnp.bfloat16)
                    s_in[t, kv, side] = middle[INNER][side].astype(jnp.bfloat16)
                    g_halo[t, side, kv] = edges[OWN][side]
                    g_out[t, kv, side] = middle[OUTER][side]
                    g_own[t, kv, side] = middle[OWN][side]

        def middle(t):
            copies = third(t)
            out, to_left, to_right = fourth(t)
            copies[2].wait_recv()
            for side in range(2):
                s_halo[t, side] = (g_halo[t, side] + r_ic[t, side].astype(jnp.float32)).astype(jnp.bfloat16)
            to_left.start()
            to_right.start()
            copies[0].wait_recv()
            copies[1].wait_recv()
            for side in range(2):
                s_out[t, :, side] = (g_out[t, :, side] + r_oc[t, 1 - side].astype(jnp.float32)).astype(jnp.bfloat16)
            out.start()

        def finish(t):
            third(t)[3].wait_recv()
            for copy in fourth(t):
                copy.wait_recv()
            for side in range(2):
                total = (
                    g_own[t, :, side]
                    + r_in[t, :, side].astype(jnp.float32)
                    + r_out[t, :, side].astype(jnp.float32)
                    + r_halo[t, 1 - side].astype(jnp.float32)
                )
                gkv_s[t, :, side] = total.astype(jnp.bfloat16)
            stores(t)[2].start()

        for t in range(NC):
            start(loads(t))
        barrier = pltpu.get_barrier_semaphore()
        for device in (to_lat(outer), to_lat(partner), to_lon(left), to_lon(right)):
            pl.semaphore_signal(barrier, inc=1, device_id=device, device_id_type=pl.DeviceIdType.MESH)
        pl.semaphore_wait(barrier, 4)
        start(first(0))
        start(first(1))
        forward(0)
        start(first(2))

        @pl.loop(0, NC)
        def _(t):
            @pl.when(t + 1 < NC)
            def _():
                forward(t + 1)

            @pl.when(t + 3 < NC)
            def _():
                start(first(t + 3))

            for copy in loads(t):
                copy.wait()
            first(t)[3].wait_recv()
            for copy in second(t):
                copy.wait_recv()
            compute(t)
            start(third(t))
            for copy in stores(t)[:2]:
                copy.start()

            @pl.when(t >= 1)
            def _():
                middle(t - 1)

            @pl.when(t >= 2)
            def _():
                finish(t - 2)

        middle(NC - 1)
        finish(NC - 2)
        finish(NC - 1)

        @pl.loop(0, NC)
        def _(t):
            for copies in (first(t), second(t), third(t), fourth(t)):
                for copy in copies:
                    copy.wait_send()
            for copy in stores(t):
                copy.wait()

    return kernel


def solution(mesh):
    kernel = make_kernel(mesh.shape["lat"], mesh.shape["lon"])
    low, full = jnp.bfloat16, jnp.float32
    pair = (NC, 2, CELLS, CH)
    quad = (NC, 2, 2, CELLS, CH)

    def body(queries, keys_values, cotangent, blocks):
        anywhere = pl.BlockSpec(memory_space=pl.ANY)
        return pl.pallas_call(
            kernel,
            out_shape=(
                jax.ShapeDtypeStruct(queries.shape, low),
                jax.ShapeDtypeStruct(queries.shape, low),
                jax.ShapeDtypeStruct(keys_values.shape, low),
            ),
            in_specs=[pl.BlockSpec(memory_space=pltpu.SMEM), anywhere, anywhere, anywhere],
            out_specs=(anywhere, anywhere, anywhere),
            scratch_shapes=[
                pltpu.VMEM((NC, 2, 3, SECTORS + 2, CELLS, CH), low),
                *[pltpu.VMEM(pair, low)] * 4,
                pltpu.VMEM(quad, low),
                *[pltpu.VMEM(quad, full)] * 3,
                *[pltpu.VMEM(quad, low)] * 10,
                pltpu.SemaphoreType.DMA((NC, 15)),
                pltpu.SemaphoreType.DMA((NC, 15)),
                pltpu.SemaphoreType.DMA((NC, 3)),
                pltpu.SemaphoreType.DMA((NC, 3)),
            ],
            compiler_params=pltpu.CompilerParams(
                collective_id=0, has_side_effects=True, vmem_limit_bytes=50 * 1024 * 1024
            ),
            cost_estimate=pl.CostEstimate(flops=4_000_000_000, bytes_accessed=4_000_000, transcendentals=1_200_000),
        )(blocks, queries, keys_values, cotangent)

    placed = (
        P("lat", "lon", None, None),
        P(None, "lat", "lon", None, None),
        P("lat", "lon", None, None),
        P("lat", "lon", None),
    )
    return jax.shard_map(
        body,
        mesh=mesh,
        in_specs=placed,
        out_specs=(placed[0], placed[0], placed[1]),
        check_vma=False,
    )
```

time: 214 us -> 58.9 us (0.28)
  local copies, waits for them, and re-layouts: 83.5 us -> 5.81 us
  matrix products: 59.7 us -> 0 us
  Pallas kernels: 0 us -> 51.5 us
  waiting for transfers between devices: 28.1 us -> 0 us
  starting transfers between devices: 25.9 us -> 0 us
  other arithmetic: 13.4 us -> 0 us
    dot_general x5 -> x0, matrix products: 52.1 us -> none  [the longest x1 21.4 us: band_attend(): jnp.einsum('bhij,bihe->bjhe', score_grad, query_heads, preferred_element_...]
    pallas_call x0 -> x1, Pallas kernels: none -> 51.5 us  [body(): pl.pallas_call(kernel, out_shape=(jax.ShapeDtypeStruct(queries.shape, low...]
    ppermute x8 -> x0, waiting for transfers between devices: 28.1 us -> none  [the longest x2 16.7 us: shifted(): return lax.ppermute(value, axis, pairs)]
    ppermute x8 -> x0, starting transfers between devices: 25.9 us -> none  [the longest x2 9.17 us: passed_along(): lax.ppermute(value, axis, [(source, source + steps) for source in range(f...]
    slice x22 -> x0, local copies, waits for them, and re-layouts: 25.3 us -> none  [the longest x12 14.7 us: body(): extended[0, dr, dc:dc + sector_cols]]
    reshape x2 -> x0, local copies, waits for them, and re-layouts: 17.7 us -> none  [the longest x1 8.88 us: band_attend(): grad_value.reshape(sector_cols, 9, CELLS, D)]
    transpose x2 -> x0, local copies, waits for them, and re-layouts: 17.1 us -> none  [the longest x1 8.53 us: band_attend(): jnp.einsum('bhij,bihe->bjhe', weights_low, upstream_heads, preferred_elem...]
    concatenate x3 -> x0, local copies, waits for them, and re-layouts: 12 us -> none  [the longest x1 6.68 us: body(): jnp.concatenate([extended[0, dr, dc:dc + sector_cols] for dr in range(3)...]
  transfers between devices with their start and end apart: 8 -> 0, of which waited for: 5 -> 0; matrix products, arithmetic and copies ran while one was open for 22% -> 0% of each run, Pallas kernels for 0% -> 0%
where the time goes in v1:
time: 58.9 us; the launch traced here: 58 us
  Pallas kernels  51.5 us (87%)
  local copies, waits for them, and re-layouts  5.81 us (10%)
  between operations  0.65 us (1%)
    pallas_call x1, Pallas kernels, body(): pl.pallas_call(kernel, out_shape=(jax.ShapeDtypeStruct(queries.shape, low...  51.5 us
    unnamed x11, local copies, waits for them, and re-layouts  5.81 us

profile of v1, /device:TPU:25, one launch (start us, length us, event | category | flops | bytes accessed | tf_op | source)
XLA Modules:
  0.0 58.0 jit_solution(17200714896825651546)
XLA Ops:
  0.6 0.0 copy-start
  0.6 1.0 %copy-done = bf16[2,1,2,64,1024]{4,3,2,1,0:T(8,128)(2,1)S(1)} copy-done((bf16[2,1,2,64,1024]{4,3,2,1,0:T(8,128)(2,1)S(1)}, bf16[2,1,2,64,1024]{4,3,2,1,0:T(8,128)(2,1)}, u32[]{:S(2)}) %copy-start) | copy-done | bytes 524312
  1.7 0.0 copy-start.1
  1.7 0.9 %copy-done.1 = bf16[1,2,64,1024]{3,2,1,0:T(8,128)(2,1)S(1)} copy-done((bf16[1,2,64,1024]{3,2,1,0:T(8,128)(2,1)S(1)}, bf16[1,2,64,1024]{3,2,1,0:T(8,128)(2,1)}, u32[]{:S(2)}) %copy-start.1) | copy-done | bytes 262168
  2.6 0.0 copy-start.2
  2.6 0.9 %copy-done.2 = bf16[1,2,64,1024]{3,2,1,0:T(8,128)(2,1)S(1)} copy-done((bf16[1,2,64,1024]{3,2,1,0:T(8,128)(2,1)S(1)}, bf16[1,2,64,1024]{3,2,1,0:T(8,128)(2,1)}, u32[]{:S(2)}) %copy-start.2) | copy-done | bytes 262168
  3.6 0.0 copy-start.3
  3.6 0.7 %copy-done.3 = s32[1,2,6]{2,1,0:T(2,128)S(1)} copy-done((s32[1,2,6]{2,1,0:T(2,128)S(1)}, s32[1,2,6]{2,1,0:T(2,128)}, u32[]{:S(2)}) %copy-start.3) | copy-done | bytes 72
  4.3 51.5 %shard_map.67 = (bf16[1,2,64,1024]{3,2,1,0:T(8,128)(2,1)S(1)}, bf16[1,2,64,1024]{3,2,1,0:T(8,128)(2,1)S(1)}, bf16[2,1,2,64,1024]{4,3,2,1,0:T(8,128)(2,1)S(1)}) custom-call(s32[1,2,6]{2,1,0:T(2,128)S(1)} %copy-done.3, bf16[1,2,64,1024]{3,2,1,0:T(8,128)(2,1)S(1)} %copy-done.1, bf16[2,1,2,64,1024]{4,3,2,1,0:T(8,128)(2,1)S(1)} %copy-done, ...), custom_call_target="tpu_custom_call" | custom-call | flops 4000000000 | bytes 4000000 | tf_op jit(solution)/shard_map/pallas_call | solution.py:272
  55.8 0.7 %copy.10 = bf16[1,2,64,1024]{3,2,1,0:T(8,128)(2,1)} copy(bf16[1,2,64,1024]{3,2,1,0:T(8,128)(2,1)S(1)} %get-tuple-element.6) | data formatting | bytes 524288
  56.5 0.7 %copy.11 = bf16[1,2,64,1024]{3,2,1,0:T(8,128)(2,1)} copy(bf16[1,2,64,1024]{3,2,1,0:T(8,128)(2,1)S(1)} %get-tuple-element.7) | data formatting | bytes 524288
  57.2 0.8 %copy.12 = bf16[2,1,2,64,1024]{4,3,2,1,0:T(8,128)(2,1)} copy(bf16[2,1,2,64,1024]{4,3,2,1,0:T(8,128)(2,1)S(1)} %get-tuple-element.8) | data formatting | bytes 1048576
Async XLA Ops:
  0.6 1.0 %copy-start = (bf16[2,1,2,64,1024]{4,3,2,1,0:T(8,128)(2,1)S(1)}, bf16[2,1,2,64,1024]{4,3,2,1,0:T(8,128)(2,1)}, u32[]{:S(2)}) copy-start(bf16[2,1,2,64,1024]{4,3,2,1,0:T(8,128)(2,1)} %kv_hbm.1) | copy-start | bytes 1572868
  1.7 0.9 %copy-start.1 = (bf16[1,2,64,1024]{3,2,1,0:T(8,128)(2,1)S(1)}, bf16[1,2,64,1024]{3,2,1,0:T(8,128)(2,1)}, u32[]{:S(2)}) copy-start(bf16[1,2,64,1024]{3,2,1,0:T(8,128)(2,1)} %q_hbm.1) | copy-start | bytes 786436
  2.6 0.9 %copy-start.2 = (bf16[1,2,64,1024]{3,2,1,0:T(8,128)(2,1)S(1)}, bf16[1,2,64,1024]{3,2,1,0:T(8,128)(2,1)}, u32[]{:S(2)}) copy-start(bf16[1,2,64,1024]{3,2,1,0:T(8,128)(2,1)} %do_hbm.1) | copy-start | bytes 786436
  3.6 0.7 %copy-start.3 = (s32[1,2,6]{2,1,0:T(2,128)S(1)}, s32[1,2,6]{2,1,0:T(2,128)}, u32[]{:S(2)}) copy-start(s32[1,2,6]{2,1,0:T(2,128)} %blocks.1) | copy-start | bytes 148

commit v2 on v1

v2 whole, which is shorter than its diff:
```python
import jax
import jax.numpy as jnp
from jax import lax
from jax.experimental import pallas as pl
from jax.experimental.pallas import tpu as pltpu
from jax.sharding import PartitionSpec as P

HEAD_DIM = 64
CELLS = 64
D = 1024
CH = 256
STEPS = D // CH
PER = CH // HEAD_DIM
NC = 2
N = STEPS // NC
SECTORS = 2
SAMPLES = 6
OUTER, OWN, INNER = 0, 1, 2
SEEN = ((0, 2, 3), (2, 3, 1))
HIDE = -1e30


def dot(a, b, ca, cb):
    return lax.dot_general(a, b, (((ca,), (cb,)), ((), ())), preferred_element_type=jnp.float32)


def make_kernel(n_lat, n_lon):
    sector_total = n_lon * SECTORS

    def kernel(
        blocks, q_hbm, kv_hbm, do_hbm, att_hbm, gq_hbm, gkv_hbm,
        ext, qs, dos, att_s, gq_s, gkv_s, g_own, g_out, g_halo,
        s_oc, s_in, s_out, s_halo, r_oc, r_yc, r_in, r_out, r_halo,
        send_sem, recv_sem, load_sem, store_sem,
    ):
        i = lax.axis_index("lat")
        j = lax.axis_index("lon")
        core = lax.rem(i, 2)
        partner = i + 1 - 2 * core
        half = n_lat // 2
        edge = (i == 0) | (i == n_lat - 1)
        seam = (i == half - 1) | (i == half)
        inside = jnp.logical_not(edge)
        plain = inside & jnp.logical_not(seam)
        beside = plain & (i >= half - 3) & (i <= half + 2)
        by_lon = (inside & jnp.logical_not(beside), seam)
        by_lat = (beside, plain)
        outer = jnp.where(edge, partner, i + 2 * core - 1)
        values_to = jnp.where(i == half - 1, 0, jnp.where(i == half, n_lat - 1, outer))
        values_to = jnp.where(i == 0, half, jnp.where(i == n_lat - 1, half - 1, values_to))
        values_from = jnp.where(i == half - 1, n_lat - 1, jnp.where(i == half, 0, outer))
        values_from = jnp.where(i == 0, half - 1, jnp.where(i == n_lat - 1, half, values_from))
        left = lax.rem(j + n_lon - 1, n_lon)
        right = lax.rem(j + 1, n_lon)

        def cols(u):
            return pl.ds(u * CH, CH)

        def loads(u):
            return [
                pltpu.make_async_copy(kv_hbm.at[0, 0, :, :, cols(u)], ext.at[u // N, OWN, 2:4, 0, u % N], load_sem.at[u, 0]),
                pltpu.make_async_copy(kv_hbm.at[1, 0, :, :, cols(u)], ext.at[u // N, OWN, 2:4, 1, u % N], load_sem.at[u, 1]),
                pltpu.make_async_copy(q_hbm.at[0, :, :, cols(u)], qs.at[u], load_sem.at[u, 2]),
                pltpu.make_async_copy(do_hbm.at[0, :, :, cols(u)], dos.at[u], load_sem.at[u, 3]),
            ]

        def stores(u):
            return [
                pltpu.make_async_copy(att_s.at[u], att_hbm.at[0, :, :, cols(u)], store_sem.at[u, 0]),
                pltpu.make_async_copy(gq_s.at[u], gq_hbm.at[0, :, :, cols(u)], store_sem.at[u, 1]),
                pltpu.make_async_copy(gkv_s.at[u, :, 0], gkv_hbm.at[0, 0, :, :, cols(u)], store_sem.at[u, 2]),
                pltpu.make_async_copy(gkv_s.at[u, :, 1], gkv_hbm.at[1, 0, :, :, cols(u)], store_sem.at[u, 3]),
            ]

        def remote(t, kind, src, dst, device, when=None):
            def make():
                return pltpu.make_async_remote_copy(
                    src_ref=src, dst_ref=dst, send_sem=send_sem.at[t, kind], recv_sem=recv_sem.at[t, kind],
                    device_id=device, device_id_type=pl.DeviceIdType.MESH,
                )

            return when, make

        def to_lat(where):
            return (where, j)

        def to_lon(where):
            return (i, where)

        def owners(t, kind, src, dst):
            return {
                "o": remote(t, kind, src, dst, to_lat(outer), plain),
                "ok": remote(t, kind, src.at[:, 0], dst.at[:, 0], to_lat(outer), seam),
                "ov": remote(t, kind + 1, src.at[:, 1], dst.at[:, 1], to_lat(values_to), seam),
                "relay": remote(t, kind + 1, dst.at[:, 1], dst.at[:, 1], to_lat(values_to), edge),
            }

        def first(t):
            own = ext.at[t, OWN]
            return {
                **owners(t, 0, own.at[2:4], ext.at[t, OUTER, 2:4]),
                "left": remote(t, 2, own.at[2], own.at[1], to_lon(left)),
                "right": remote(t, 3, own.at[3], own.at[0], to_lon(right)),
                "in": remote(t, 4, own.at[2:4], ext.at[t, INNER, 2:4], to_lat(partner)),
            }

        def second(t):
            near, far, across = ext.at[t, OWN], ext.at[t, OUTER], ext.at[t, INNER]
            found = {"in": remote(t, 5, near.at[0:2], across.at[0:2], to_lat(partner))}
            for kv in range(2):
                found["left", kv] = remote(t, 6 + kv, far.at[2, kv], far.at[1, kv], to_lon(left), by_lon[kv])
                found["right", kv] = remote(t, 8 + kv, far.at[3, kv], far.at[0, kv], to_lon(right), by_lon[kv])
                found["out", kv] = remote(t, 10 + kv, near.at[0:2, kv], far.at[0:2, kv], to_lat(outer), by_lat[kv])
            return found

        def third(t):
            found = {"in": remote(t, 12, s_in.at[t], r_in.at[t], to_lat(partner))}
            for kv in range(2):
                found["left", kv] = remote(t, 13 + kv, s_oc.at[t, 0, kv], r_oc.at[t, 0, kv], to_lon(left), by_lon[kv])
                found["right", kv] = remote(t, 15 + kv, s_oc.at[t, 1, kv], r_oc.at[t, 1, kv], to_lon(right), by_lon[kv])
                found["out", kv] = remote(t, 17 + kv, s_oc.at[t, :, kv], r_yc.at[t, :, kv], to_lat(outer), by_lat[kv])
            return found

        def fourth(t):
            return {
                **owners(t, 19, s_out.at[t], r_out.at[t]),
                "left": remote(t, 21, s_halo.at[t, 0], r_halo.at[t, 0], to_lon(left)),
                "right": remote(t, 22, s_halo.at[t, 1], r_halo.at[t, 1], to_lon(right)),
            }

        def each(make, t, names, act):
            copies = [make(t)[name] for name in names]
            while copies:
                when = copies[0][0]
                same = [copy for copy in copies if copy[0] is when]
                copies = [copy for copy in copies if copy[0] is not when]

                def run():
                    for _, copy in same:
                        act(copy())

                if when is None:
                    run()
                else:
                    pl.when(when)(run)

        def start(make, t, names):
            each(make, t, names, lambda copy: copy.start())

        def arrived(make, t, names):
            each(make, t, names, lambda copy: copy.wait_recv())

        def arrived_values(make, t):
            @pl.when(jnp.logical_not(plain))
            def _():
                make(t)["ov"][1]().wait_recv()

            start(make, t, ["relay"])

        sides = [(side, kv) for kv in range(2) for side in ("left", "right")]
        outs = [("out", 0), ("out", 1)]

        def forward(t):
            arrived(first, t, ["left", "right"])
            start(second, t, ["in", *outs])
            arrived(first, t, ["o", "ok"])
            start(second, t, sides[:2])
            arrived_values(first, t)
            start(second, t, sides[2:])

        sign = 1 - 2 * core
        bias = []
        for b in range(SECTORS):
            codes = []
            for s in range(SAMPLES):
                block = blocks[0, b, s]
                band = block // sector_total
                sector = block % sector_total
                column = (sector - (SECTORS * j + b) + 1 + sector_total) % sector_total
                codes.append((1 + sign * (band - i)) * 3 + column)
            row = []
            for o in range(9):
                listed = codes[0] == o
                for code in codes[1:]:
                    listed = listed | (code == o)
                row.append(jnp.where(listed, 0.0, HIDE).astype(jnp.float32))
            bias.append(row)

        head = lax.broadcasted_iota(jnp.int32, (CELLS, CH), 1) // HEAD_DIM
        on = [jnp.where(head == h, 1.0, 0.0).astype(jnp.float32) for h in range(PER)]
        on_low = [o.astype(jnp.bfloat16) for o in on]

        def spread(x):
            return jnp.concatenate([x * m for m in on_low], axis=0)

        def gathered(x):
            total = x[0:CELLS] * on[0]
            for h in range(1, PER):
                total = total + x[h * CELLS : (h + 1) * CELLS] * on[h]
            return total

        def compute(t, n):
            u = t * N + n
            scale = HEAD_DIM ** -0.5
            grads = ([], [])
            for b in range(SECTORS):
                qbd = spread(qs[u, b])
                dbd = spread(dos[u, b])
                keys = jnp.concatenate([ext[t, r, c, 0, n] for r in range(3) for c in SEEN[b]], axis=0)
                values = jnp.concatenate([ext[t, r, c, 1, n] for r in range(3) for c in SEEN[b]], axis=0)
                scores = dot(keys, qbd, 1, 1)
                scores = jnp.concatenate(
                    [scores[o * CELLS : (o + 1) * CELLS] + bias[b][o] for o in range(9)], axis=0
                )
                highest = jnp.max(scores, axis=0, keepdims=True)
                raised = jnp.exp((scores - highest) * scale)
                weights = raised * (1.0 / jnp.sum(raised, axis=0, keepdims=True))
                low = weights.astype(jnp.bfloat16)
                pressure = dot(values, dbd, 1, 1)
                inner = jnp.sum(weights * pressure, axis=0, keepdims=True)
                score_grad = (weights * (pressure - inner) * scale).astype(jnp.bfloat16)
                att_s[u, b] = gathered(dot(low, values, 0, 0)).astype(jnp.bfloat16)
                gq_s[u, b] = gathered(dot(score_grad, keys, 0, 0)).astype(jnp.bfloat16)
                grads[0].append(dot(score_grad, qbd, 1, 0).reshape(3, 3, CELLS, CH))
                grads[1].append(dot(low, dbd, 1, 0).reshape(3, 3, CELLS, CH))
            for kv in range(2):
                g0, g1 = grads[kv]
                for r in range(3):
                    edges = (g0[r, 0], g1[r, 2])
                    middle = (g0[r, 1] + g1[r, 0], g0[r, 2] + g1[r, 1])
                    for side in range(2):
                        if r == INNER:
                            s_in[t, side, kv, n] = edges[side].astype(jnp.bfloat16)
                            s_in[t, 2 + side, kv, n] = middle[side].astype(jnp.bfloat16)
                        elif r == OUTER:
                            s_oc[t, side, kv, n] = edges[side].astype(jnp.bfloat16)
                            g_out[u, side, kv] = middle[side]
                        else:
                            g_halo[u, side, kv] = edges[side]
                            g_own[u, side, kv] = middle[side]

        def middle(t):
            arrived(third, t, ["in", *outs])

            @pl.loop(0, N)
            def _(n):
                for side in range(2):
                    total = g_halo[t * N + n, side] + r_in[t, side, :, n].astype(jnp.float32)
                    s_halo[t, side, :, n] = (total + r_yc[t, side, :, n].astype(jnp.float32)).astype(jnp.bfloat16)

            start(fourth, t, ["left", "right"])
            arrived(third, t, sides)

            @pl.loop(0, N)
            def _(n):
                for side in range(2):
                    total = g_out[t * N + n, side] + r_oc[t, 1 - side, :, n].astype(jnp.float32)
                    s_out[t, side, :, n] = total.astype(jnp.bfloat16)

            start(fourth, t, ["o", "ok", "ov"])

        def finish(t):
            arrived(fourth, t, ["o", "ok"])
            arrived_values(fourth, t)
            arrived(fourth, t, ["left", "right"])

            @pl.loop(0, N)
            def _(n):
                for side in range(2):
                    total = (
                        g_own[t * N + n, side]
                        + r_in[t, 2 + side, :, n].astype(jnp.float32)
                        + jnp.where(inside, r_out[t, side, :, n].astype(jnp.float32), 0.0)
                        + r_halo[t, 1 - side, :, n].astype(jnp.float32)
                    )
                    gkv_s[t * N + n, side] = total.astype(jnp.bfloat16)

            for u in range(t * N, t * N + N):
                for copy in stores(u)[2:]:
                    copy.start()

        for u in range(STEPS):
            for copy in loads(u)[:2]:
                copy.start()
        for u in range(STEPS):
            for copy in loads(u)[2:]:
                copy.start()

        def greet(device):
            pl.semaphore_signal(barrier, inc=1, device_id=device, device_id_type=pl.DeviceIdType.MESH)

        barrier = pltpu.get_barrier_semaphore()
        for device in (to_lat(partner), to_lon(left), to_lon(right), to_lat(values_to)):
            greet(device)

        @pl.when(edge)
        def _():
            greet(to_lat(values_from))

        @pl.when(seam)
        def _():
            greet(to_lat(values_from))
            greet(to_lat(outer))

        def clear(when, ref, *at):
            @pl.when(when)
            def _():
                @pl.loop(0, NC)
                def _(t):
                    ref[(t, *at)] = jnp.zeros(ref.shape[1 + len(at) :], ref.dtype)

        for place in range(4):
            clear(edge, ext, OUTER, place, 0)
        for side in range(2):
            clear(edge, ext, OUTER, side, 1)
            clear(edge, r_out, side, 0)
            for kv in range(2):
                clear(jnp.logical_not(by_lon[kv]), r_oc, side, kv)
                clear(jnp.logical_not(by_lat[kv]), r_yc, side, kv)
        for u in range(STEPS):
            for copy in loads(u)[:2]:
                copy.wait()

        for when, peers in ((plain, 4), (edge, 5), (seam, 6)):

            @pl.when(when)
            def _():
                pl.semaphore_wait(barrier, peers)

        for t in range(NC):
            start(first, t, ["left", "right", "o", "ok", "ov", "in"])
        forward(0)
        for u in range(STEPS):
            for copy in loads(u)[2:]:
                copy.wait()
        for t in range(NC):
            if t + 1 < NC:
                forward(t + 1)
            arrived(first, t, ["in"])
            arrived(second, t, ["in", *sides, *outs])

            @pl.loop(0, N)
            def _(n):
                compute(t, n)

            start(third, t, ["in", *sides, *outs])
            for u in range(t * N, t * N + N):
                for copy in stores(u)[:2]:
                    copy.start()
            if t >= 1:
                middle(t - 1)
            if t >= 2:
                finish(t - 2)
        middle(NC - 1)
        if NC > 1:
            finish(NC - 2)
        finish(NC - 1)
        for t in range(NC):
            for make in (first, second, third, fourth):
                each(make, t, list(make(t)), lambda copy: copy.wait_send())
        for u in range(STEPS):
            for copy in stores(u):
                copy.wait()

    return kernel


def hand_over(*refs):
    copies = [pltpu.make_async_copy(refs[k], refs[3 + k], refs[6].at[k]) for k in range(3)]
    for copy in copies:
        copy.start()
    for copy in copies:
        copy.wait()


def solution(mesh):
    kernel = make_kernel(mesh.shape["lat"], mesh.shape["lon"])
    low, full = jnp.bfloat16, jnp.float32
    pair = (STEPS, 2, CELLS, CH)
    quad = (STEPS, 2, 2, CELLS, CH)
    sent = (NC, 2, 2, N, CELLS, CH)
    wide = (NC, 4, 2, N, CELLS, CH)

    def body(queries, keys_values, cotangent, blocks):
        far = pl.BlockSpec(memory_space=pltpu.HBM)
        results = pl.pallas_call(
            kernel,
            out_shape=(
                jax.ShapeDtypeStruct(queries.shape, low),
                jax.ShapeDtypeStruct(queries.shape, low),
                jax.ShapeDtypeStruct(keys_values.shape, low),
            ),
            in_specs=[pl.BlockSpec(memory_space=pltpu.SMEM), far, far, far],
            out_specs=(far, far, far),
            scratch_shapes=[
                pltpu.VMEM((NC, 3, 4, 2, N, CELLS, CH), low),
                *[pltpu.VMEM(pair, low)] * 4,
                pltpu.VMEM(quad, low),
                *[pltpu.VMEM(quad, full)] * 3,
                pltpu.VMEM(sent, low),
                pltpu.VMEM(wide, low),
                *[pltpu.VMEM(sent, low)] * 4,
                pltpu.VMEM(wide, low),
                *[pltpu.VMEM(sent, low)] * 2,
                pltpu.SemaphoreType.DMA((NC, 23)),
                pltpu.SemaphoreType.DMA((NC, 23)),
                pltpu.SemaphoreType.DMA((STEPS, 4)),
                pltpu.SemaphoreType.DMA((STEPS, 4)),
            ],
            compiler_params=pltpu.CompilerParams(
                collective_id=0, has_side_effects=True, vmem_limit_bytes=62 * 1024 * 1024
            ),
            cost_estimate=pl.CostEstimate(flops=4_000_000_000, bytes_accessed=4_000_000, transcendentals=1_200_000),
        )(blocks, queries, keys_values, cotangent)
        return pl.pallas_call(
            hand_over,
            out_shape=tuple(jax.ShapeDtypeStruct(r.shape, r.dtype) for r in results),
            in_specs=[pl.BlockSpec(memory_space=pltpu.VMEM)] * 3,
            out_specs=(far,) * 3,
            scratch_shapes=[pltpu.SemaphoreType.DMA((3,))],
        )(*results)

    placed = (
        P("lat", "lon", None, None),
        P(None, "lat", "lon", None, None),
        P("lat", "lon", None, None),
        P("lat", "lon", None),
    )
    return jax.shard_map(
        body,
        mesh=mesh,
        in_specs=placed,
        out_specs=(placed[0], placed[0], placed[1]),
        check_vma=False,
    )
```

time: 58.9 us -> 49.7 us (0.84); the launches traced: 58 us -> 49.5 us
  local copies, waits for them, and re-layouts: 5.81 us -> 0 us
  Pallas kernels: 51.5 us -> 48.9 us
    unnamed x11 -> x0, local copies, waits for them, and re-layouts: 5.81 us -> none
    pallas_call x1, Pallas kernels: 51.5 us -> 46.7 us  [body(): pl.pallas_call(kernel, out_shape=(jax.ShapeDtypeStruct(queries.shape, low...]
    pallas_call x0 -> x1, Pallas kernels: none -> 2.19 us  [body(): pl.pallas_call(hand_over, out_shape=tuple((jax.ShapeDtypeStruct(r.shape,...]
where the time goes in v2:
time: 49.7 us; the launch traced here: 49.5 us
  Pallas kernels  48.9 us (98%)
  between operations  0.64 us (1%)
    pallas_call x1, Pallas kernels, body(): pl.pallas_call(kernel, out_shape=(jax.ShapeDtypeStruct(queries.shape, low...  46.7 us
    pallas_call x1, Pallas kernels, body(): pl.pallas_call(hand_over, out_shape=tuple((jax.ShapeDtypeStruct(r.shape,...  2.19 us

profile of v2, /device:TPU:25, one launch (start us, length us, event | category | flops | bytes accessed | tf_op | source)
XLA Modules:
  0.0 49.5 jit_solution(8745291091740201230)
XLA Ops:
  0.6 46.7 %shard_map.67 = (bf16[1,2,64,1024]{3,2,1,0:T(8,128)(2,1)}, bf16[1,2,64,1024]{3,2,1,0:T(8,128)(2,1)}, bf16[2,1,2,64,1024]{4,3,2,1,0:T(8,128)(2,1)}) custom-call(s32[1,2,6]{2,1,0:T(2,128)} %blocks.1, bf16[1,2,64,1024]{3,2,1,0:T(8,128)(2,1)} %q_hbm.1, bf16[2,1,2,64,1024]{4,3,2,1,0:T(8,128)(2,1)} %kv_hbm.1, bf16[1,2,64,1024]{3,2,1,0:T(8,128)(2,1)} %do_hbm.1), custom_call_target="tpu_custom_call" | custom-call | flops 4000000000 | bytes 4000000 | tf_op jit(solution)/shard_map/pallas_call | solution.py:386
  47.3 2.2 %shard_map.68 = (bf16[1,2,64,1024]{3,2,1,0:T(8,128)(2,1)}, bf16[1,2,64,1024]{3,2,1,0:T(8,128)(2,1)}, bf16[2,1,2,64,1024]{4,3,2,1,0:T(8,128)(2,1)}) custom-call(bf16[1,2,64,1024]{3,2,1,0:T(8,128)(2,1)} %get-tuple-element.6.refs_0_, bf16[1,2,64,1024]{3,2,1,0:T(8,128)(2,1)} %get-tuple-element.7.refs_1_, bf16[2,1,2,64,1024]{4,3,2,1,0:T(8,128)(2,1)} %get-tuple-element.8.refs_2_), custom_call_target="tpu_custom_call" | custom-call | tf_op jit(solution)/shard_map/pallas_call | solution.py:415

commit v3 on v2

--- a/solution.py
+++ b/solution.py
@@ -16,8 +16,6 @@
 SECTORS = 2
 SAMPLES = 6
 OUTER, OWN, INNER = 0, 1, 2
-SEEN = ((0, 2, 3), (2, 3, 1))
-HIDE = -1e30
 
 
 def dot(a, b, ca, cb):
@@ -31,7 +29,7 @@
         blocks, q_hbm, kv_hbm, do_hbm, att_hbm, gq_hbm, gkv_hbm,
         ext, qs, dos, att_s, gq_s, gkv_s, g_own, g_out, g_halo,
         s_oc, s_in, s_out, s_halo, r_oc, r_yc, r_in, r_out, r_halo,
-        send_sem, recv_sem, load_sem, store_sem,
+        near, grads, send_sem, recv_sem, load_sem, store_sem,
     ):
         i = lax.axis_index("lat")
         j = lax.axis_index("lon")
@@ -105,12 +103,12 @@
             }
 
         def second(t):
-            near, far, across = ext.at[t, OWN], ext.at[t, OUTER], ext.at[t, INNER]
-            found = {"in": remote(t, 5, near.at[0:2], across.at[0:2], to_lat(partner))}
+            home, far, across = ext.at[t, OWN], ext.at[t, OUTER], ext.at[t, INNER]
+            found = {"in": remote(t, 5, home.at[0:2], across.at[0:2], to_lat(partner))}
             for kv in range(2):
                 found["left", kv] = remote(t, 6 + kv, far.at[2, kv], far.at[1, kv], to_lon(left), by_lon[kv])
                 found["right", kv] = remote(t, 8 + kv, far.at[3, kv], far.at[0, kv], to_lon(right), by_lon[kv])
-                found["out", kv] = remote(t, 10 + kv, near.at[0:2, kv], far.at[0:2, kv], to_lat(outer), by_lat[kv])
+                found["out", kv] = remote(t, 10 + kv, home.at[0:2, kv], far.at[0:2, kv], to_lat(outer), by_lat[kv])
             return found
 
         def third(t):
@@ -150,12 +148,16 @@
         def arrived(make, t, names):
             each(make, t, names, lambda copy: copy.wait_recv())
 
-        def arrived_values(make, t):
-            @pl.when(jnp.logical_not(plain))
+        def pass_on(make, t):
+            @pl.when(edge)
             def _():
                 make(t)["ov"][1]().wait_recv()
-
-            start(make, t, ["relay"])
+                make(t)["relay"][1]().start()
+
+        def arrived_values(make, t):
+            @pl.when(seam)
+            def _():
+                make(t)["ov"][1]().wait_recv()
 
         sides = [(side, kv) for kv in range(2) for side in ("left", "right")]
         outs = [("out", 0), ("out", 1)]
@@ -165,26 +167,34 @@
             start(second, t, ["in", *outs])
             arrived(first, t, ["o", "ok"])
             start(second, t, sides[:2])
+            pass_on(first, t)
             arrived_values(first, t)
             start(second, t, sides[2:])
 
         sign = 1 - 2 * core
-        bias = []
+        listed, slot = [], []
         for b in range(SECTORS):
-            codes = []
+            codes, row = [], []
             for s in range(SAMPLES):
                 block = blocks[0, b, s]
                 band = block // sector_total
                 sector = block % sector_total
                 column = (sector - (SECTORS * j + b) + 1 + sector_total) % sector_total
-                codes.append((1 + sign * (band - i)) * 3 + column)
+                role = 1 + sign * (band - i)
+                codes.append(role * 3 + column)
+                place = jnp.where(column == 0, 0, column + 1) if b == 0 else jnp.where(column == 2, 1, column + 2)
+                row.append(jnp.minimum(jnp.maximum(role * 4 + place, 0), 11))
+            listed.append(row)
             row = []
             for o in range(9):
-                listed = codes[0] == o
-                for code in codes[1:]:
-                    listed = listed | (code == o)
-                row.append(jnp.where(listed, 0.0, HIDE).astype(jnp.float32))
-            bias.append(row)
+                found = SAMPLES
+                for s in range(SAMPLES):
+                    found = jnp.where(codes[s] == o, s, found)
+                row.append(found)
+            slot.append(row)
+        for b in range(SECTORS):
+            for kv in range(2):
+                grads[b, kv, SAMPLES] = jnp.zeros((CELLS, CH), jnp.float32)
 
         head = lax.broadcasted_iota(jnp.int32, (CELLS, CH), 1) // HEAD_DIM
         on = [jnp.where(head == h, 1.0, 0.0).astype(jnp.float32) for h in range(PER)]
@@ -202,16 +212,15 @@
         def compute(t, n):
             u = t * N + n
             scale = HEAD_DIM ** -0.5
-            grads = ([], [])
+            for r in range(3):
+                for c in range(4):
+                    near[r * 4 + c] = ext[t, r, c, :, n]
             for b in range(SECTORS):
                 qbd = spread(qs[u, b])
                 dbd = spread(dos[u, b])
-                keys = jnp.concatenate([ext[t, r, c, 0, n] for r in range(3) for c in SEEN[b]], axis=0)
-                values = jnp.concatenate([ext[t, r, c, 1, n] for r in range(3) for c in SEEN[b]], axis=0)
+                keys = jnp.concatenate([near[block, 0] for block in listed[b]], axis=0)
+                values = jnp.concatenate([near[block, 1] for block in listed[b]], axis=0)
                 scores = dot(keys, qbd, 1, 1)
-                scores = jnp.concatenate(
-                    [scores[o * CELLS : (o + 1) * CELLS] + bias[b][o] for o in range(9)], axis=0
-                )
                 highest = jnp.max(scores, axis=0, keepdims=True)
                 raised = jnp.exp((scores - highest) * scale)
                 weights = raised * (1.0 / jnp.sum(raised, axis=0, keepdims=True))
@@ -221,13 +230,14 @@
                 score_grad = (weights * (pressure - inner) * scale).astype(jnp.bfloat16)
                 att_s[u, b] = gathered(dot(low, values, 0, 0)).astype(jnp.bfloat16)
                 gq_s[u, b] = gathered(dot(score_grad, keys, 0, 0)).astype(jnp.bfloat16)
-                grads[0].append(dot(score_grad, qbd, 1, 0).reshape(3, 3, CELLS, CH))
-                grads[1].append(dot(low, dbd, 1, 0).reshape(3, 3, CELLS, CH))
+                for kv, grad in enumerate((dot(score_grad, qbd, 1, 0), dot(low, dbd, 1, 0))):
+                    for s in range(SAMPLES):
+                        grads[b, kv, s] = grad[s * CELLS : (s + 1) * CELLS]
             for kv in range(2):
-                g0, g1 = grads[kv]
                 for r in range(3):
-                    edges = (g0[r, 0], g1[r, 2])
-                    middle = (g0[r, 1] + g1[r, 0], g0[r, 2] + g1[r, 1])
+                    g0, g1 = [[grads[b, kv, slot[b][3 * r + c]] for c in range(3)] for b in range(SECTORS)]
+                    edges = (g0[0], g1[2])
+                    middle = (g0[1] + g1[0], g0[2] + g1[1])
                     for side in range(2):
                         if r == INNER:
                             s_in[t, side, kv, n] = edges[side].astype(jnp.bfloat16)
@@ -327,17 +337,16 @@
             def _():
                 pl.semaphore_wait(barrier, peers)
 
-        for t in range(NC):
+        def send(t):
             start(first, t, ["left", "right", "o", "ok", "ov", "in"])
-        forward(0)
-        for u in range(STEPS):
-            for copy in loads(u)[2:]:
-                copy.wait()
-        for t in range(NC):
-            if t + 1 < NC:
-                forward(t + 1)
+
+        def work(t):
             arrived(first, t, ["in"])
             arrived(second, t, ["in", *sides, *outs])
+            if t == 0:
+                for u in range(STEPS):
+                    for copy in loads(u)[2:]:
+                        copy.wait()
 
             @pl.loop(0, N)
             def _(n):
@@ -347,14 +356,19 @@
             for u in range(t * N, t * N + N):
                 for copy in stores(u)[:2]:
                     copy.start()
-            if t >= 1:
-                middle(t - 1)
-            if t >= 2:
-                finish(t - 2)
-        middle(NC - 1)
-        if NC > 1:
-            finish(NC - 2)
-        finish(NC - 1)
+
+        send(0)
+        send(1)
+        forward(0)
+        forward(1)
+        work(0)
+        work(1)
+        middle(0)
+        pass_on(fourth, 0)
+        middle(1)
+        pass_on(fourth, 1)
+        finish(0)
+        finish(1)
         for t in range(NC):
             for make in (first, second, third, fourth):
                 each(make, t, list(make(t)), lambda copy: copy.wait_send())
@@ -366,10 +380,15 @@
 
 
 def hand_over(*refs):
-    copies = [pltpu.make_async_copy(refs[k], refs[3 + k], refs[6].at[k]) for k in range(3)]
-    for copy in copies:
+    sources, results, held, sem = refs[:3], refs[3:6], refs[6:9], refs[9]
+    loads = [pltpu.make_async_copy(sources[k], held[k], sem.at[0, k]) for k in range(3)]
+    stores = [pltpu.make_async_copy(held[k], results[k], sem.at[1, k]) for k in range(3)]
+    for copy in loads:
         copy.start()
-    for copy in copies:
+    for load, store in zip(loads, stores):
+        load.wait()
+        store.start()
+    for copy in stores:
         copy.wait()
 
 
@@ -402,6 +421,8 @@
                 *[pltpu.VMEM(sent, low)] * 4,
                 pltpu.VMEM(wide, low),
                 *[pltpu.VMEM(sent, low)] * 2,
+                pltpu.VMEM((12, 2, CELLS, CH), low),
+                pltpu.VMEM((SECTORS, 2, SAMPLES + 1, CELLS, CH), full),
                 pltpu.SemaphoreType.DMA((NC, 23)),
                 pltpu.SemaphoreType.DMA((NC, 23)),
                 pltpu.SemaphoreType.DMA((STEPS, 4)),
@@ -415,9 +436,10 @@
         return pl.pallas_call(
             hand_over,
             out_shape=tuple(jax.ShapeDtypeStruct(r.shape, r.dtype) for r in results),
-            in_specs=[pl.BlockSpec(memory_space=pltpu.VMEM)] * 3,
+            in_specs=[far] * 3,
             out_specs=(far,) * 3,
-            scratch_shapes=[pltpu.SemaphoreType.DMA((3,))],
+            scratch_shapes=[*[pltpu.VMEM(r.shape, r.dtype) for r in results], pltpu.SemaphoreType.DMA((2, 3))],
+            compiler_params=pltpu.CompilerParams(vmem_limit_bytes=62 * 1024 * 1024),
         )(*results)
 
     placed = (

time: 49.7 us -> 48.8 us (0.982)
  Pallas kernels: 48.9 us -> 47.7 us
    pallas_call x1, Pallas kernels: 46.7 us -> 45.6 us  [body(): pl.pallas_call(kernel, out_shape=(jax.ShapeDtypeStruct(queries.shape, low...]
where the time goes in v3:
time: 48.8 us; the launch traced here: 48.3 us
  Pallas kernels  47.7 us (98%)
  between operations  0.64 us (1%)
    pallas_call x1, Pallas kernels, body(): pl.pallas_call(kernel, out_shape=(jax.ShapeDtypeStruct(queries.shape, low...  45.6 us
    pallas_call x1, Pallas kernels, body(): pl.pallas_call(hand_over, out_shape=tuple((jax.ShapeDtypeStruct(r.shape,...  2.05 us

profile of v3, /device:TPU:25, one launch (start us, length us, event | category | flops | bytes accessed | tf_op | source)
XLA Modules:
  0.0 48.3 jit_solution(2309323246257141003)
XLA Ops:
  0.6 45.6 %shard_map.67 = (bf16[1,2,64,1024]{3,2,1,0:T(8,128)(2,1)}, bf16[1,2,64,1024]{3,2,1,0:T(8,128)(2,1)}, bf16[2,1,2,64,1024]{4,3,2,1,0:T(8,128)(2,1)}) custom-call(s32[1,2,6]{2,1,0:T(2,128)} %blocks.1, bf16[1,2,64,1024]{3,2,1,0:T(8,128)(2,1)} %q_hbm.1, bf16[2,1,2,64,1024]{4,3,2,1,0:T(8,128)(2,1)} %kv_hbm.1, bf16[1,2,64,1024]{3,2,1,0:T(8,128)(2,1)} %do_hbm.1), custom_call_target="tpu_custom_call" | custom-call | flops 4000000000 | bytes 4000000 | tf_op jit(solution)/shard_map/pallas_call | solution.py:405
  46.3 2.0 %shard_map.68 = (bf16[1,2,64,1024]{3,2,1,0:T(8,128)(2,1)}, bf16[1,2,64,1024]{3,2,1,0:T(8,128)(2,1)}, bf16[2,1,2,64,1024]{4,3,2,1,0:T(8,128)(2,1)}) custom-call(bf16[1,2,64,1024]{3,2,1,0:T(8,128)(2,1)} %get-tuple-element.6.refs_0_, bf16[1,2,64,1024]{3,2,1,0:T(8,128)(2,1)} %get-tuple-element.7.refs_1_, bf16[2,1,2,64,1024]{4,3,2,1,0:T(8,128)(2,1)} %get-tuple-element.8.refs_2_), custom_call_target="tpu_custom_call" | custom-call | tf_op jit(solution)/shard_map/pallas_call | solution.py:436

commit v4 on v3

--- a/solution.py
+++ b/solution.py
@@ -51,6 +51,28 @@
         left = lax.rem(j + n_lon - 1, n_lon)
         right = lax.rem(j + 1, n_lon)
 
+        def to_lat(where):
+            return (where, j)
+
+        def to_lon(where):
+            return (i, where)
+
+        def greet(device):
+            pl.semaphore_signal(barrier, inc=1, device_id=device, device_id_type=pl.DeviceIdType.MESH)
+
+        barrier = pltpu.get_barrier_semaphore()
+        for device in (to_lat(partner), to_lon(left), to_lon(right), to_lat(values_to)):
+            greet(device)
+
+        @pl.when(edge)
+        def _():
+            greet(to_lat(values_from))
+
+        @pl.when(seam)
+        def _():
+            greet(to_lat(values_from))
+            greet(to_lat(outer))
+
         def cols(u):
             return pl.ds(u * CH, CH)
 
@@ -70,6 +92,13 @@
                 pltpu.make_async_copy(gkv_s.at[u, :, 1], gkv_hbm.at[1, 0, :, :, cols(u)], store_sem.at[u, 3]),
             ]
 
+        for u in range(STEPS):
+            for copy in loads(u)[:2]:
+                copy.start()
+        for u in range(STEPS):
+            for copy in loads(u)[2:]:
+                copy.start()
+
         def remote(t, kind, src, dst, device, when=None):
             def make():
                 return pltpu.make_async_remote_copy(
@@ -78,12 +107,6 @@
                 )
 
             return when, make
-
-        def to_lat(where):
-            return (where, j)
-
-        def to_lon(where):
-            return (i, where)
 
         def owners(t, kind, src, dst):
             return {
@@ -289,29 +312,6 @@
                 for copy in stores(u)[2:]:
                     copy.start()
 
-        for u in range(STEPS):
-            for copy in loads(u)[:2]:
-                copy.start()
-        for u in range(STEPS):
-            for copy in loads(u)[2:]:
-                copy.start()
-
-        def greet(device):
-            pl.semaphore_signal(barrier, inc=1, device_id=device, device_id_type=pl.DeviceIdType.MESH)
-
-        barrier = pltpu.get_barrier_semaphore()
-        for device in (to_lat(partner), to_lon(left), to_lon(right), to_lat(values_to)):
-            greet(device)
-
-        @pl.when(edge)
-        def _():
-            greet(to_lat(values_from))
-
-        @pl.when(seam)
-        def _():
-            greet(to_lat(values_from))
-            greet(to_lat(outer))
-
         def clear(when, ref, *at):
             @pl.when(when)
             def _():
@@ -327,9 +327,6 @@
             for kv in range(2):
                 clear(jnp.logical_not(by_lon[kv]), r_oc, side, kv)
                 clear(jnp.logical_not(by_lat[kv]), r_yc, side, kv)
-        for u in range(STEPS):
-            for copy in loads(u)[:2]:
-                copy.wait()
 
         for when, peers in ((plain, 4), (edge, 5), (seam, 6)):
 
@@ -338,6 +335,9 @@
                 pl.semaphore_wait(barrier, peers)
 
         def send(t):
+            for u in range(t * N, t * N + N):
+                for copy in loads(u)[:2]:
+                    copy.wait()
             start(first, t, ["left", "right", "o", "ok", "ov", "in"])
 
         def work(t):

time: 48.8 us -> 48.5 us (level)
  no operation moved by 1% of the time
where the time goes in v4:
time: 48.5 us; the launch traced here: 48.1 us
  Pallas kernels  47.4 us (98%)
  between operations  0.64 us (1%)
    pallas_call x1, Pallas kernels, body(): pl.pallas_call(kernel, out_shape=(jax.ShapeDtypeStruct(queries.shape, low...  45.4 us
    pallas_call x1, Pallas kernels, body(): pl.pallas_call(hand_over, out_shape=tuple((jax.ShapeDtypeStruct(r.shape,...  2.05 us

profile of v4, /device:TPU:25, one launch (start us, length us, event | category | flops | bytes accessed | tf_op | source)
XLA Modules:
  0.0 48.1 jit_solution(11984204366222308659)
XLA Ops:
  0.6 45.4 %shard_map.67 = (bf16[1,2,64,1024]{3,2,1,0:T(8,128)(2,1)}, bf16[1,2,64,1024]{3,2,1,0:T(8,128)(2,1)}, bf16[2,1,2,64,1024]{4,3,2,1,0:T(8,128)(2,1)}) custom-call(s32[1,2,6]{2,1,0:T(2,128)} %blocks.1, bf16[1,2,64,1024]{3,2,1,0:T(8,128)(2,1)} %q_hbm.1, bf16[2,1,2,64,1024]{4,3,2,1,0:T(8,128)(2,1)} %kv_hbm.1, bf16[1,2,64,1024]{3,2,1,0:T(8,128)(2,1)} %do_hbm.1), custom_call_target="tpu_custom_call" | custom-call | flops 4000000000 | bytes 4000000 | tf_op jit(solution)/shard_map/pallas_call | solution.py:405
  46.0 2.0 %shard_map.68 = (bf16[1,2,64,1024]{3,2,1,0:T(8,128)(2,1)}, bf16[1,2,64,1024]{3,2,1,0:T(8,128)(2,1)}, bf16[2,1,2,64,1024]{4,3,2,1,0:T(8,128)(2,1)}) custom-call(bf16[1,2,64,1024]{3,2,1,0:T(8,128)(2,1)} %get-tuple-element.6.refs_0_, bf16[1,2,64,1024]{3,2,1,0:T(8,128)(2,1)} %get-tuple-element.7.refs_1_, bf16[2,1,2,64,1024]{4,3,2,1,0:T(8,128)(2,1)} %get-tuple-element.8.refs_2_), custom_call_target="tpu_custom_call" | custom-call | tf_op jit(solution)/shard_map/pallas_call | solution.py:436
